TPU v7x, 512 devices: a whole 4x4x16 slice. The times are simulated.
512 devices in a mesh: basin: 64 (over z, x), reach: 8 (over y, core).
Axes of the slice: x: 4, y: 4, z: 16, core: 2. Of those that a mesh axis runs over, the one named last changes fastest.
Arguments:
- reach_residual: float32 [384, 24, 128], P('basin', 'reach'), may hold values from -4 to 4
- chain_inv: float32 [384, 24, 128, 128], P('basin', 'reach'), may hold values from -1 to 2
- chain_link: float32 [384, 24, 128, 128], P('basin', 'reach'), may hold values from -1 to 1
- outlet_link: float32 [384, 128, 128], P('basin'), may hold values from -0.5 to 0.5
- junction_inv: float32 [384, 128, 128], P('basin'), may hold values from -1 to 1
- junction_residual: float32 [384, 128], P('basin'), may hold values from -6 to 6
- upper_junction: int32 [384], P('basin'), may hold values from 0 to 383
- lower_junction: int32 [384], P('basin'), may hold values from 0 to 383
- cell_cotangent: float32 [384, 24, 128], P('basin', 'reach'), may hold values from -4 to 4
- junction_cotangent: float32 [384, 128], P('basin'), may hold values from -6 to 6
Outputs:
- cell_update: float32 [384, 24, 128], P('basin', 'reach')
- section_update: float32 [384, 128], P('basin')
- cell_adjoint: float32 [384, 24, 128], P('basin', 'reach')
- junction_adjoint: float32 [384, 128], P('basin')
Inputs may be any that keep to these rules, and one draw needn't show every extreme that they name: `upper_junction`: junction ids. `lower_junction`: junction ids.
All inputs are finite; a program needn't handle non-finite values.
Results may differ from a plain program's by a relative error of at most 0.00014.
Values sent between devices are 32-bit elements; how exact they have to be, the bound alone decides.
No kernel may reach another device: no remote copies, remote signals or barrier semaphores. Data moves between devices by JAX's collectives and lax.ppermute only.
A program may use at most 64 MiB of HBM per device.

v0:
```python
import jax
import jax.numpy as jnp
from jax import lax
from jax.sharding import PartitionSpec as P

SWEEPS = 4
precise = lax.Precision.HIGHEST


def entering(x, axis, combine, identity, reverse):
    length, place = (lax.axis_size(axis), lax.axis_index(axis))
    everything = jax.tree.map(lambda part: lax.all_gather(part, axis), x)
    start = jax.tree.map(
        lambda part, zero: jnp.broadcast_to(jnp.asarray(zero, part.dtype), part.shape), x, identity
    )

    def lap(k, before):
        at = length - 1 - k if reverse else k
        reached = at > place if reverse else at < place
        new = combine(before, jax.tree.map(lambda part: part[at], everything))
        return jax.tree.map(lambda a, b: jnp.where(reached, a, b), new, before)

    return lax.fori_loop(0, length, lap, start)


def from_root(block, axis, holder):
    block = jnp.where(lax.axis_index(axis) == holder, block, jnp.zeros_like(block))
    return lax.psum(block, axis)


def product(former, latter):
    return jnp.einsum("sij,sjk->sik", former, latter, precision=precise)


def applied(matrix, vector):
    return jnp.einsum("sij,sj->si", matrix, vector, precision=precise)


def applied_transposed(matrix, vector):
    return jnp.einsum("sji,sj->si", matrix, vector, precision=precise)


def compose(former, latter):
    return (product(latter[0], former[0]), applied(latter[0], former[1]) + latter[1])


def identity_map(members, tile_width):
    eye_block = jnp.broadcast_to(
        jnp.eye(tile_width, dtype=jnp.float32), (members, tile_width, tile_width)
    )
    return (eye_block, jnp.zeros((members, tile_width), jnp.float32))


def entry_maps(local_map, neutral):
    return entering(local_map, "reach", compose, neutral, False)


def exit_maps(local_map, neutral):
    return entering(local_map, "reach", compose, neutral, True)


def shards(
    reach_residual,
    chain_inv,
    chain_link,
    outlet_link,
    junction_inv,
    junction_residual,
    upper_junction,
    lower_junction,
    cell_cotangent,
    junction_cotangent,
):
    members, blocks, tile_width = reach_residual.shape
    owned_rows = junction_inv.shape[0]
    junctions = owned_rows * lax.axis_size("basin")
    final_reach = lax.axis_size("reach") - 1
    multiplier = jnp.einsum("skij,skjl->skil", chain_inv, chain_link, precision=precise)
    forced = jnp.einsum("skij,skj->ski", chain_inv, reach_residual, precision=precise)
    local_matrix = multiplier[:, 0]
    local_vector = forced[:, 0]
    for number in range(1, blocks):
        local_matrix = product(multiplier[:, number], local_matrix)
        local_vector = applied(multiplier[:, number], local_vector) + forced[:, number]
    neutral = identity_map(members, tile_width)
    entry_map = entry_maps((local_matrix, local_vector), neutral)
    outlet = compose(entry_map, (local_matrix, local_vector))
    schur_tile = product(outlet_link, outlet[0])
    outlet_push = applied(outlet_link, outlet[1])
    schur_tile, outlet_push = (
        from_root(schur_tile, "reach", final_reach),
        from_root(outlet_push, "reach", final_reach),
    )
    backward = cell_cotangent[:, blocks - 1]
    for number in range(blocks - 2, -1, -1):
        backward = cell_cotangent[:, number] + applied_transposed(
            multiplier[:, number + 1], backward
        )
    local_back = applied_transposed(multiplier[:, 0], backward)
    reverse_local = (jnp.swapaxes(local_matrix, 1, 2), local_back)
    leaving = exit_maps(reverse_local, neutral)
    head_value = applied(reverse_local[0], leaving[1]) + local_back
    upward = from_root(head_value, "reach", 0)
    junction_rows = jnp.arange(junctions, dtype=jnp.int32)[:, None]
    lower_onehot = (junction_rows == lower_junction[None, :]).astype(jnp.float32)
    upper_onehot = (junction_rows == upper_junction[None, :]).astype(jnp.float32)

    def section_terms(section_all):
        return outlet_push + applied(schur_tile, section_all[upper_junction])

    def adjoint_terms(relief_all):
        return upward + applied_transposed(schur_tile, relief_all[lower_junction])

    sections = jnp.zeros((owned_rows, tile_width), jnp.float32)
    adjoint = jnp.zeros((owned_rows, tile_width), jnp.float32)

    def gather_sections(values):
        return lax.all_gather(values, "basin", axis=0, tiled=True)

    def gather_relief(values):
        return lax.all_gather(values, "basin", axis=0, tiled=True)

    for sweep_index in range(SWEEPS):
        inflow_terms = outlet_push if sweep_index == 0 else section_terms(gather_sections(sections))
        placed = jnp.dot(lower_onehot, inflow_terms, precision=precise)
        inflow = lax.psum_scatter(placed, "basin", scatter_dimension=0, tiled=True)
        sections = applied(junction_inv, junction_residual + inflow)
    for sweep_index in range(SWEEPS):
        return_terms = (
            upward
            if sweep_index == 0
            else adjoint_terms(gather_relief(applied_transposed(junction_inv, adjoint)))
        )
        placed = jnp.dot(upper_onehot, return_terms, precision=precise)
        adjoint = junction_cotangent + lax.psum_scatter(
            placed, "basin", scatter_dimension=0, tiled=True
        )
    section_all = gather_sections(sections)
    relief_all = gather_relief(applied_transposed(junction_inv, adjoint))
    head_sections = section_all[upper_junction]
    tail_relief = relief_all[lower_junction]
    carried = applied(entry_map[0], head_sections) + entry_map[1]
    cell_rows = []
    for number in range(blocks):
        carried = applied(multiplier[:, number], carried) + forced[:, number]
        cell_rows.append(carried)
    cell_update = jnp.stack(cell_rows, axis=1)
    incoming = applied_transposed(outlet_link, tail_relief)
    carried = cell_cotangent[:, blocks - 1] + applied(leaving[0], incoming) + leaving[1]
    collected = [carried]
    for number in range(blocks - 2, -1, -1):
        carried = cell_cotangent[:, number] + applied_transposed(multiplier[:, number + 1], carried)
        collected.append(carried)
    cell_adjoint = jnp.stack(collected[::-1], axis=1)
    return (cell_update, sections, cell_adjoint, adjoint)


def solution(mesh):
    placed = (
        P("basin", "reach", None),
        P("basin", "reach", None, None),
        P("basin", "reach", None, None),
        P("basin", None, None),
        P("basin", None, None),
        P("basin", None),
        P("basin"),
        P("basin"),
        P("basin", "reach", None),
        P("basin", None),
    )
    return jax.shard_map(
        shards,
        mesh=mesh,
        in_specs=placed,
        out_specs=(
            P("basin", "reach", None),
            P("basin", None),
            P("basin", "reach", None),
            P("basin", None),
        ),
        check_vma=False,
    )
```

profile of v0, /device:TPU:8, one launch (start us, length us, event | category | flops | bytes accessed | tf_op | source)
XLA Modules:
  0.0 1940.1 jit_solution(3543780025443325133)
XLA Ops:
  8.4 2.5 fusion.138
  15.3 16.4 all-gather.9
  31.7 1.9 fusion.48
  35.1 13.7 all-gather.4
  52.1 32.2 %while.35 = (s32[]{:T(128)}, f32[6,128,128]{2,1,0:T(8,128)S(1)}, f32[6,128]{1,0:T(8,128)S(1)}, s32[]{:T(128)}, f32[8,6,128,128]{3,2,1,0:T(8,128)}, /*index=5*/f3...) while((s32[]{:T(128)}, f32[6,128,128]{2,1,0:T(8,128)S(1)}, ...), condition=%wide.region_9.10_spmd.clone, body=%wide.region_8.9_spmd.clone.sunk | while | flops 152275968 | bytes 2777269 | solution.py:23
  52.1 1.7 fusion.194
  72.2 1.7 fusion.194
  80.3 1.7 fusion.194
  85.3 4.5 all-gather.17.cloned.1.call-done
  90.7 32.1 %while.34 = (s32[]{:T(128)}, f32[6,128,128]{2,1,0:T(8,128)S(1)}, f32[6,128]{1,0:T(8,128)S(1)}, s32[]{:T(128)}, f32[8,6,128,128]{3,2,1,0:T(8,128)}, /*index=5*/f32[8,6,128]{2,1,0:T(8,128)}, s32[]{:T(128)}, s32[]{:T(128)}) while((s32[]{:T(128)}, f32[6,128,128]{2,1,0:T(8,128)S(1)}, f32[6,128]{1,0:T(8,128)S(1)}, s32[]{:T(128)}, ...), condition=%wide.region_1.2_spmd.clone, body=%wide.region_0.1_spmd.clone.sunk | while | flops 152275968 | bytes 2778223 | solution.py:23
  126.6 12.1 all-reduce.12
  142.2 1.8 fusion.139
  144.1 2.7 fusion.18
  146.8 261.6 %all-reduce.27.cloned.1.call-done = (f32[384,128]{1,0:T(8,128)}, f32[384,128]{1,0:T(8,128)}) async-done(((f32[384,128]{1,0:T(8,128)}, f32[384,128]{1,0:T(8,128)}), (f32[384,128]{1,0:T(8,128)}, f32[384,128]{1,0:T(8,128)})) %all-reduce.27.cloned.1.call-update) | async-done | bytes 393232
  410.2 85.1 %all-gather.10 = f32[64,6,128]{2,1,0:T(8,128)} all-gather(f32[1,6,128]{2,1,0:T(8,128)S(1)} %bitcast.365), channel_id=1, replica_groups=mesh['basin'=64,'reach'=8] {'basin'}, dimensions={0}, use_global_device_ids=true | all-gather | bytes 199680 | tf_op jit(solution)/shard_map/all_gather | solution.py:121
  497.0 2.2 gather_fusion.4
  503.9 86.5 %all-gather.5 = f32[64,6,128]{2,1,0:T(8,128)} all-gather(f32[1,6,128]{2,1,0:T(8,128)S(1)} %bitcast.366), channel_id=1, replica_groups=mesh['basin'=64,'reach'=8] {'basin'}, dimensions={0}, use_global_device_ids=true | all-gather | bytes 199680 | tf_op jit(solution)/shard_map/all_gather | solution.py:118
  592.1 2.2 gather_fusion
  597.4 259.3 %all-reduce.25.cloned.1.call-done = (f32[384,128]{1,0:T(8,128)}, f32[384,128]{1,0:T(8,128)}) async-done(((f32[384,128]{1,0:T(8,128)}, f32[384,128]{1,0:T(8,128)}), (f32[384,128]{1,0:T(8,128)}, f32[384,128]{1,0:T(8,128)})) %all-reduce.25.cloned.1.call-update) | async-done | bytes 393232
  857.8 85.1 %all-gather.11 = f32[64,6,128]{2,1,0:T(8,128)} all-gather(f32[1,6,128]{2,1,0:T(8,128)S(1)} %bitcast.367), channel_id=1, replica_groups=mesh['basin'=64,'reach'=8] {'basin'}, dimensions={0}, use_global_device_ids=true | all-gather | bytes 199680 | tf_op jit(solution)/shard_map/all_gather | solution.py:121
  944.5 2.2 gather_fusion.5
  951.5 86.5 %all-gather.6 = f32[64,6,128]{2,1,0:T(8,128)} all-gather(f32[1,6,128]{2,1,0:T(8,128)S(1)} %bitcast.368), channel_id=1, replica_groups=mesh['basin'=64,'reach'=8] {'basin'}, dimensions={0}, use_global_device_ids=true | all-gather | bytes 199680 | tf_op jit(solution)/shard_map/all_gather | solution.py:118
  1039.6 2.2 gather_fusion.1
  1044.9 259.3 %all-reduce.23.cloned.1.call-done = (f32[384,128]{1,0:T(8,128)}, f32[384,128]{1,0:T(8,128)}) async-done(((f32[384,128]{1,0:T(8,128)}, f32[384,128]{1,0:T(8,128)}), (f32[384,128]{1,0:T(8,128)}, f32[384,128]{1,0:T(8,128)})) %all-reduce.23.cloned.1.call-update) | async-done | bytes 393232
  1305.4 85.1 %all-gather.12 = f32[64,6,128]{2,1,0:T(8,128)} all-gather(f32[1,6,128]{2,1,0:T(8,128)S(1)} %bitcast.369), channel_id=1, replica_groups=mesh['basin'=64,'reach'=8] {'basin'}, dimensions={0}, use_global_device_ids=true | all-gather | bytes 199680 | tf_op jit(solution)/shard_map/all_gather | solution.py:121
  1392.2 2.2 gather_fusion.6
  1399.2 86.7 %all-gather.7 = f32[64,6,128]{2,1,0:T(8,128)} all-gather(f32[1,6,128]{2,1,0:T(8,128)S(1)} %bitcast.370), channel_id=1, replica_groups=mesh['basin'=64,'reach'=8] {'basin'}, dimensions={0}, use_global_device_ids=true | all-gather | bytes 199680 | tf_op jit(solution)/shard_map/all_gather | solution.py:118
  1487.5 2.2 gather_fusion.2
  1492.8 259.4 %all-reduce.21.cloned.1.call-done = (f32[384,128]{1,0:T(8,128)}, f32[384,128]{1,0:T(8,128)}) async-done(((f32[384,128]{1,0:T(8,128)}, f32[384,128]{1,0:T(8,128)}), (f32[384,128]{1,0:T(8,128)}, f32[384,128]{1,0:T(8,128)})) %all-reduce.21.cloned.1.call-update) | async-done | bytes 393232
  1753.9 85.1 %all-gather.13 = f32[64,6,128]{2,1,0:T(8,128)} all-gather(f32[1,6,128]{2,1,0:T(8,128)S(1)} %bitcast.371), channel_id=1, replica_groups=mesh['basin'=64,'reach'=8] {'basin'}, dimensions={0}, use_global_device_ids=true | all-gather | bytes 199680 | tf_op jit(solution)/shard_map/all_gather | solution.py:121
  1840.6 2.2 gather_fusion.7
  1848.0 81.0 %all-gather.8 = f32[64,6,128]{2,1,0:T(8,128)S(1)} all-gather(f32[1,6,128]{2,1,0:T(8,128)S(1)} %bitcast.363), channel_id=1, replica_groups=mesh['basin'=64,'reach'=8] {'basin'}, dimensions={0}, use_global_device_ids=true | all-gather | bytes 199680 | tf_op jit(solution)/shard_map/all_gather | solution.py:118
  (240 shorter events, 127.4 us)
Async XLA Ops:
  7.2 1.3 copy-start
  7.2 44.8 %all-gather.19.cloned.1.call-start = ((), (), s32[]{:S(2)}) async-start(), calls=%async_computation.2 | async-start | bytes 3538944 | tf_op jit(solution)/shard_map/all_gather | solution.py:12
  11.5 2.3 copy-start.23
  12.0 1.0 copy-start.2
  13.0 18.8 copy-start.22
  13.0 76.8 %all-gather.17.cloned.1.call-start = ((), (), s32[]{:S(2)}) async-start(), calls=%async_computation.1 | async-start | bytes 3538944 | tf_op jit(solution)/shard_map/all_gather | solution.py:12
  13.7 394.7 %all-reduce.27.cloned.1.call-start = ((), (), s32[]{:S(2)}) async-start(), calls=%async_computation.6 | async-start | bytes 786432
  13.8 38.2 %copy-start.4 = (f32[128,128]{1,0:T(8,128)}, f32[128,128]{1,0:T(8,128)S(1)}, u32[]{:S(2)}) copy-start(f32[128,128]{1,0:T(8,128)S(1)} %fusion.47) | copy-start | bytes 196612
  13.9 17.8 copy-start.12
  13.9 17.8 copy-start.14
  13.9 17.8 copy-start.16
  14.8 34.0 %copy-start.21 = (s32[6]{0:T(128)S(1)}, s32[6]{0:T(128)}, u32[]{:S(2)}) copy-start(s32[6]{0:T(128)} %param.21) | copy-start | bytes 76
  14.8 34.6 %copy-start.20 = (s32[6]{0:T(128)S(1)}, s32[6]{0:T(128)}, u32[]{:S(2)}) copy-start(s32[6]{0:T(128)} %param.20) | copy-start | bytes 76
  33.7 18.4 copy-start.5
  35.1 17.0 copy-start.11
  52.1 32.2 %copy-start.3 = (f32[6,128,128]{2,1,0:T(8,128)S(1)}, f32[6,128,128]{2,1,0:T(8,128)}, u32[]{:S(2)}) copy-start(f32[6,128,128]{2,1,0:T(8,128)} %copy-done.2) | copy-start | bytes 1179652
  138.7 3.4 copy-start.9
  138.8 3.4 copy-start.10
  141.9 357.2 %all-reduce.19.cloned.1.call-start = ((), (), s32[]{:S(2)}) async-start(), calls=%async_computation | async-start | bytes 786432 | tf_op jit(solution)/shard_map/psum | solution.py:28
  142.2 266.2 %copy-start.7 = (f32[6,128]{1,0:T(8,128)S(1)}, f32[6,128]{1,0:T(8,128)}, u32[]{:S(2)}) copy-start(f32[6,128]{1,0:T(8,128)} %param.23) | copy-start | bytes 9220
  142.2 266.2 %copy-start.8 = (f32[6,128]{1,0:T(8,128)S(1)}, f32[6,128]{1,0:T(8,128)}, u32[]{:S(2)}) copy-start(f32[6,128]{1,0:T(8,128)} %param.19) | copy-start | bytes 9220
  142.2 267.5 %copy-start.1 = (f32[6,128,128]{2,1,0:T(8,128)S(1)}, f32[6,128,128]{2,1,0:T(8,128)}, u32[]{:S(2)}) copy-start(f32[6,128,128]{2,1,0:T(8,128)} %param.18) | copy-start | bytes 1179652
  146.8 709.9 %all-reduce.25.cloned.1.call-start = ((), (), s32[]{:S(2)}) async-start(), calls=%async_computation.5 | async-start | bytes 786432
  597.3 707.0 %all-reduce.23.cloned.1.call-start = ((), (), s32[]{:S(2)}) async-start(), calls=%async_computation.4 | async-start | bytes 786432
  1044.9 707.3 %all-reduce.21.cloned.1.call-start = ((), (), s32[]{:S(2)}) async-start(), calls=%async_computation.3 | async-start | bytes 786432
  1752.9 0.6 copy-start.19
  1752.9 92.1 %copy-start.13 = (f32[6,1,128]{2,1,0:T(1,128)S(1)}, f32[6,1,128]{2,1,0:T(1,128)}, u32[]{:S(2)}) copy-start(f32[6,1,128]{2,1,0:T(1,128)} %copy-done.12) | copy-start | bytes 9220
  1842.8 2.6 copy-start.15
  1842.8 3.1 copy-start.17
  1845.5 85.7 %copy-start.6 = (f32[6,3,1,128]{3,0,1,2:T(8,128)S(1)}, f32[6,3,1,128]{3,0,1,2:T(8,128)}, u32[]{:S(2)}) copy-start(f32[6,3,1,128]{3,0,1,2:T(8,128)} %copy-done.5) | copy-start | bytes 27652
  1848.0 84.6 %copy-start.18 = (f32[6,1,128]{2,0,1:T(8,128)}, f32[6,1,128]{2,0,1:T(8,128)S(1)}, u32[]{:S(2)}) copy-start(f32[6,1,128]{2,0,1:T(8,128)S(1)} %copy.279) | copy-start | bytes 9220
Sparse Core Ops, SparseCore 0:
  13.1 38.8 all-gather.18
  54.1 35.6 all-gather.16
  142.1 266.3 all-reduce.26
  410.6 68.1 all-reduce.18
  597.5 259.1 all-reduce.24
  1045.0 259.2 all-reduce.22
  1492.9 259.2 all-reduce.20
where the time goes:
time: 1940 us
  waiting for transfers between devices  1040 us (54%)
  blocking collectives  723 us (37%)
  matrix products  102 us (5%)
  local copies, waits for them, and re-layouts  34.4 us (2%)
  other arithmetic  19.5 us (1%)
    unnamed x11, waiting for transfers between devices  1040 us
    all_gather x4, blocking collectives, gather_sections(): return lax.all_gather(values, 'basin', axis=0, tiled=True)  341 us
    all_gather x4, blocking collectives, gather_relief(): return lax.all_gather(values, 'basin', axis=0, tiled=True)  340 us
    dot_general x33, matrix products, applied(): return jnp.einsum('sij,sj->si', matrix, vector, precision=precise)  43.8 us
  transfers between devices with their start and end apart: 7, of which 5 were waited for; matrix products, arithmetic and copies ran while one was open for 3% of the time, Pallas kernels for 0%

commit v1 on v0

--- a/solution.py
+++ b/solution.py
@@ -118,7 +118,9 @@
         return lax.all_gather(values, "basin", axis=0, tiled=True)
 
     def gather_relief(values):
-        return lax.all_gather(values, "basin", axis=0, tiled=True)
+        return jnp.concatenate(
+            lax.all_to_all(jnp.stack([values] * lax.axis_size("basin")), "basin", 0, 0), axis=0
+        )
 
     for sweep_index in range(SWEEPS):
         inflow_terms = outlet_push if sweep_index == 0 else section_terms(gather_sections(sections))

time: 1940 us -> 1660 us (0.86)
  blocking collectives: 723 us -> 393 us
  starting transfers between devices: 0.47 us -> 35.7 us
    all_gather x4 -> x0, blocking collectives: 340 us -> none  [gather_relief(): return lax.all_gather(values, 'basin', axis=0, tiled=True)]
    all_to_all x0 -> x4, starting transfers between devices: none -> 35.4 us  [gather_relief(): lax.all_to_all(jnp.stack([values] * lax.axis_size('basin')), 'basin', 0, 0)]
  transfers between devices with their start and end apart: 7 -> 11, of which waited for: 5 -> 6; matrix products, arithmetic and copies ran while one was open for 3% -> 5% of each run, Pallas kernels for 0% -> 0%
where the time goes in v1:
time: 1660 us
  waiting for transfers between devices  1050 us (63%)
  blocking collectives  393 us (24%)
  matrix products  102 us (6%)
  local copies, waits for them, and re-layouts  36.6 us (2%)
  starting transfers between devices  35.7 us (2%)
  other arithmetic  23.9 us (1%)
    unnamed x11, waiting for transfers between devices  1050 us
    all_gather x4, blocking collectives, gather_sections(): return lax.all_gather(values, 'basin', axis=0, tiled=True)  349 us
    dot_general x33, matrix products, applied(): return jnp.einsum('sij,sj->si', matrix, vector, precision=precise)  43.8 us
    all_to_all x4, starting transfers between devices, gather_relief(): lax.all_to_all(jnp.stack([values] * lax.axis_size('basin')), 'basin', 0, 0)  35.4 us
  transfers between devices with their start and end apart: 11, of which 6 were waited for; matrix products, arithmetic and copies ran while one was open for 5% of the time, Pallas kernels for 0%

profile of v1, /device:TPU:8, one launch (start us, length us, event | category | flops | bytes accessed | tf_op | source)
XLA Modules:
  0.0 1659.0 jit_solution(13767590875661819132)
XLA Ops:
  8.4 2.5 fusion.138
  15.3 16.3 all-gather.9
  31.6 1.9 fusion.48
  35.0 13.9 all-gather.4
  50.1 1.9 all-gather.15.cloned.1.call-done
  52.1 32.2 %while.35 = (s32[]{:T(128)}, f32[6,128,128]{2,1,0:T(8,128)S(1)}, f32[6,128]{1,0:T(8,128)S(1)}, s32[]{:T(128)}, f32[8,6,128,128]{3,2,1,0:T(8,128)}, /*index=5*/f3...) while((s32[]{:T(128)}, f32[6,128,128]{2,1,0:T(8,128)S(1)}, ...), condition=%wide.region_9.10_spmd.clone, body=%wide.region_8.9_spmd.clone.sunk | while | flops 152275968 | bytes 2777269 | solution.py:23
  52.1 1.7 fusion.194
  72.2 1.7 fusion.194
  85.3 4.4 all-gather.13.cloned.1.call-done
  90.6 32.1 %while.34 = (s32[]{:T(128)}, f32[6,128,128]{2,1,0:T(8,128)S(1)}, f32[6,128]{1,0:T(8,128)S(1)}, s32[]{:T(128)}, f32[8,6,128,128]{3,2,1,0:T(8,128)}, /*index=5*/f32[8,6,128]{2,1,0:T(8,128)}, s32[]{:T(128)}, s32[]{:T(128)}) while((s32[]{:T(128)}, f32[6,128,128]{2,1,0:T(8,128)S(1)}, f32[6,128]{1,0:T(8,128)S(1)}, s32[]{:T(128)}, ...), condition=%wide.region_1.2_spmd.clone, body=%wide.region_0.1_spmd.clone.sunk | while | flops 152275968 | bytes 2778223 | solution.py:23
  125.4 1.8 fusion.122
  127.8 13.0 all-reduce.12
  148.5 2.5 fusion.139
  151.0 259.7 %all-reduce.27.cloned.1.call-done = (f32[384,128]{1,0:T(8,128)}, f32[384,128]{1,0:T(8,128)}) async-done(((f32[384,128]{1,0:T(8,128)}, f32[384,128]{1,0:T(8,128)}), (f32[384,128]{1,0:T(8,128)}, f32[384,128]{1,0:T(8,128)})) %all-reduce.27.cloned.1.call-update) | async-done | bytes 393232
  413.2 8.9 all-to-all-start
  422.1 2.8 fusion.18
  426.4 88.7 %all-gather.5 = f32[64,6,128]{2,1,0:T(8,128)} all-gather(f32[1,6,128]{2,1,0:T(8,128)S(1)} %bitcast.362), channel_id=1, replica_groups=mesh['basin'=64,'reach'=8] {'basin'}, dimensions={0}, use_global_device_ids=true | all-gather | bytes 199680 | tf_op jit(solution)/shard_map/all_gather | solution.py:118
  516.7 2.2 gather_fusion
  523.6 2.2 gather_fusion.4
  529.2 262.0 %all-reduce.25.cloned.1.call-done = (f32[384,128]{1,0:T(8,128)}, f32[384,128]{1,0:T(8,128)}) async-done(((f32[384,128]{1,0:T(8,128)}, f32[384,128]{1,0:T(8,128)}), (f32[384,128]{1,0:T(8,128)}, f32[384,128]{1,0:T(8,128)})) %all-reduce.25.cloned.1.call-update) | async-done | bytes 393232
  793.0 8.9 all-to-all-start.1
  803.4 88.7 %all-gather.6 = f32[64,6,128]{2,1,0:T(8,128)} all-gather(f32[1,6,128]{2,1,0:T(8,128)S(1)} %bitcast.364), channel_id=1, replica_groups=mesh['basin'=64,'reach'=8] {'basin'}, dimensions={0}, use_global_device_ids=true | all-gather | bytes 199680 | tf_op jit(solution)/shard_map/all_gather | solution.py:118
  893.7 2.2 gather_fusion.1
  900.6 2.2 gather_fusion.5
  906.1 262.0 %all-reduce.23.cloned.1.call-done = (f32[384,128]{1,0:T(8,128)}, f32[384,128]{1,0:T(8,128)}) async-done(((f32[384,128]{1,0:T(8,128)}, f32[384,128]{1,0:T(8,128)}), (f32[384,128]{1,0:T(8,128)}, f32[384,128]{1,0:T(8,128)})) %all-reduce.23.cloned.1.call-update) | async-done | bytes 393232
  1170.0 8.9 all-to-all-start.2
  1180.3 88.9 %all-gather.7 = f32[64,6,128]{2,1,0:T(8,128)} all-gather(f32[1,6,128]{2,1,0:T(8,128)S(1)} %bitcast.366), channel_id=1, replica_groups=mesh['basin'=64,'reach'=8] {'basin'}, dimensions={0}, use_global_device_ids=true | all-gather | bytes 199680 | tf_op jit(solution)/shard_map/all_gather | solution.py:118
  1270.9 2.2 gather_fusion.2
  1277.7 2.2 gather_fusion.6
  1283.3 262.0 %all-reduce.21.cloned.1.call-done = (f32[384,128]{1,0:T(8,128)}, f32[384,128]{1,0:T(8,128)}) async-done(((f32[384,128]{1,0:T(8,128)}, f32[384,128]{1,0:T(8,128)}), (f32[384,128]{1,0:T(8,128)}, f32[384,128]{1,0:T(8,128)})) %all-reduce.21.cloned.1.call-update) | async-done | bytes 393232
  1547.8 8.9 all-to-all-start.3
  1558.1 83.0 %all-gather.8 = f32[64,6,128]{2,1,0:T(8,128)S(1)} all-gather(f32[1,6,128]{2,1,0:T(8,128)S(1)} %bitcast.359), channel_id=1, replica_groups=mesh['basin'=64,'reach'=8] {'basin'}, dimensions={0}, use_global_device_ids=true | all-gather | bytes 199680 | tf_op jit(solution)/shard_map/all_gather | solution.py:118
  (246 shorter events, 134.9 us)
Async XLA Ops:
  7.2 1.3 copy-start
  7.2 44.8 %all-gather.15.cloned.1.call-start = ((), (), s32[]{:S(2)}) async-start(), calls=%async_computation.6 | async-start | bytes 3538944 | tf_op jit(solution)/shard_map/all_gather | solution.py:12
  11.5 2.3 copy-start.22
  13.0 18.7 %copy-start.21 = (f32[6,3,128]{2,1,0:T(4,128)S(1)}, f32[6,3,128]{2,1,0:T(4,128)}, u32[]{:S(2)}) copy-start(f32[6,3,128]{2,1,0:T(4,128)} %param.14) | copy-start | bytes 27652
  13.0 76.7 %all-gather.13.cloned.1.call-start = ((), (), s32[]{:S(2)}) async-start(), calls=%async_computation.5 | async-start | bytes 3538944 | tf_op jit(solution)/shard_map/all_gather | solution.py:12
  13.7 396.9 %all-reduce.27.cloned.1.call-start = ((), (), s32[]{:S(2)}) async-start(), calls=%async_computation.10 | async-start | bytes 786432
  13.8 38.2 %copy-start.5 = (f32[128,128]{1,0:T(8,128)}, f32[128,128]{1,0:T(8,128)S(1)}, u32[]{:S(2)}) copy-start(f32[128,128]{1,0:T(8,128)S(1)} %fusion.47) | copy-start | bytes 196612
  13.9 17.8 %copy-start.11 = (f32[6,1,128]{2,1,0:T(1,128)}, f32[6,1,128]{2,1,0:T(1,128)S(1)}, u32[]{:S(2)}) copy-start(f32[6,1,128]{2,1,0:T(1,128)S(1)} %get-tuple-element.373) | copy-start | bytes 9220
  13.9 17.7 %copy-start.13 = (f32[6,1,128]{2,1,0:T(1,128)}, f32[6,1,128]{2,1,0:T(1,128)S(1)}, u32[]{:S(2)}) copy-start(f32[6,1,128]{2,1,0:T(1,128)S(1)} %get-tuple-element.374) | copy-start | bytes 9220
  13.9 17.7 %copy-start.15 = (f32[6,1,128]{2,1,0:T(1,128)}, f32[6,1,128]{2,1,0:T(1,128)S(1)}, u32[]{:S(2)}) copy-start(f32[6,1,128]{2,1,0:T(1,128)S(1)} %get-tuple-element.375) | copy-start | bytes 9220
  14.8 34.2 %copy-start.19 = (s32[6]{0:T(128)S(1)}, s32[6]{0:T(128)}, u32[]{:S(2)}) copy-start(s32[6]{0:T(128)} %param.21) | copy-start | bytes 76
  14.8 34.7 %copy-start.20 = (s32[6]{0:T(128)S(1)}, s32[6]{0:T(128)}, u32[]{:S(2)}) copy-start(s32[6]{0:T(128)} %param.20) | copy-start | bytes 76
  33.6 18.5 %copy-start.6 = (f32[6,3,1,128]{3,0,1,2:T(8,128)}, f32[6,3,1,128]{3,0,1,2:T(8,128)S(1)}, u32[]{:S(2)}) copy-start(f32[6,3,1,128]{3,0,1,2:T(8,128)S(1)} %copy.276) | copy-start | bytes 27652
  35.0 17.0 %copy-start.10 = (f32[6,1,128]{2,1,0:T(1,128)}, f32[6,1,128]{2,1,0:T(1,128)S(1)}, u32[]{:S(2)}) copy-start(f32[6,1,128]{2,1,0:T(1,128)S(1)} %fusion.25) | copy-start | bytes 9220
  52.0 32.2 %copy-start.3 = (f32[6,128,128]{2,1,0:T(8,128)S(1)}, f32[6,128,128]{2,1,0:T(8,128)}, u32[]{:S(2)}) copy-start(f32[6,128,128]{2,1,0:T(8,128)} %copy-done.2) | copy-start | bytes 1179652
  125.4 285.3 %copy-start.8 = (f32[6,128]{1,0:T(8,128)S(1)}, f32[6,128]{1,0:T(8,128)}, u32[]{:S(2)}) copy-start(f32[6,128]{1,0:T(8,128)} %param.23) | copy-start | bytes 9220
  125.4 285.3 %copy-start.9 = (f32[6,128]{1,0:T(8,128)S(1)}, f32[6,128]{1,0:T(8,128)}, u32[]{:S(2)}) copy-start(f32[6,128]{1,0:T(8,128)} %param.19) | copy-start | bytes 9220
  125.4 286.6 %copy-start.1 = (f32[6,128,128]{2,1,0:T(8,128)S(1)}, f32[6,128,128]{2,1,0:T(8,128)}, u32[]{:S(2)}) copy-start(f32[6,128,128]{2,1,0:T(8,128)} %param.18) | copy-start | bytes 1179652
  413.2 108.8 %all-to-all-start = ((f32[64,6,128]{2,1,0:T(8,128)}), f32[64,6,128]{2,1,0:T(8,128)}, u32[]{:S(2)}, u32[]{:S(2)}) async-start(f32[64,6,128]{2,1,0:T(8,128)} %stack.28), calls=%async_computation | async-start | bytes 524288 | tf_op jit(solution)/shard_map/all_to_all | solution.py:122
  422.0 96.9 %all-reduce.19.cloned.1.call-start = ((), (), s32[]{:S(2)}) async-start(), calls=%async_computation.4 | async-start | bytes 786432 | tf_op jit(solution)/shard_map/psum | solution.py:28
  424.9 366.3 %all-reduce.25.cloned.1.call-start = ((), (), s32[]{:S(2)}) async-start(), calls=%async_computation.9 | async-start | bytes 786432
  793.0 105.9 %all-to-all-start.1 = ((f32[64,6,128]{2,1,0:T(8,128)}), f32[64,6,128]{2,1,0:T(8,128)}, u32[]{:S(2)}, u32[]{:S(2)}) async-start(f32[64,6,128]{2,1,0:T(8,128)} %stack.29), calls=%async_computation.1 | async-start | bytes 524288 | tf_op jit(solution)/shard_map/all_to_all | solution.py:122
  801.9 366.2 %all-reduce.23.cloned.1.call-start = ((), (), s32[]{:S(2)}) async-start(), calls=%async_computation.8 | async-start | bytes 786432
  1170.0 106.1 %all-to-all-start.2 = ((f32[64,6,128]{2,1,0:T(8,128)}), f32[64,6,128]{2,1,0:T(8,128)}, u32[]{:S(2)}, u32[]{:S(2)}) async-start(f32[64,6,128]{2,1,0:T(8,128)} %stack.30), calls=%async_computation.2 | async-start | bytes 524288 | tf_op jit(solution)/shard_map/all_to_all | solution.py:122
  1178.8 366.5 %all-reduce.21.cloned.1.call-start = ((), (), s32[]{:S(2)}) async-start(), calls=%async_computation.7 | async-start | bytes 786432
  1547.8 100.0 %all-to-all-start.3 = ((f32[64,6,128]{2,1,0:T(8,128)}), f32[64,6,128]{2,1,0:T(8,128)}, u32[]{:S(2)}, u32[]{:S(2)}) async-start(f32[64,6,128]{2,1,0:T(8,128)} %stack.31), calls=%async_computation.3 | async-start | bytes 524288 | tf_op jit(solution)/shard_map/all_to_all | solution.py:122
  1558.1 89.0 %copy-start.17 = (f32[6,1,128]{2,0,1:T(8,128)}, f32[6,1,128]{2,0,1:T(8,128)S(1)}, u32[]{:S(2)}) copy-start(f32[6,1,128]{2,0,1:T(8,128)S(1)} %copy.279) | copy-start | bytes 9220
  1641.8 7.6 copy-start.4
  1643.5 2.9 copy-start.7
  1644.9 5.6 copy-start.12
  1646.4 4.7 copy-start.14
  1647.1 4.4 copy-start.16
  (2 other events, 1.6 us)
Sparse Core Ops, SparseCore 0:
  13.1 38.8 all-gather.14
  54.1 35.5 all-gather.12
  144.2 266.4 all-reduce.26
  425.0 74.3 all-reduce.18
  529.3 261.8 all-reduce.24
  906.2 261.8 all-reduce.22
  1283.4 261.8 all-reduce.20
